TPU v7x, 32 devices: a whole 2x2x4 slice. The times are simulated.
32 devices in a mesh: gx: 4 (over z), gy: 4 (over y, x), layer: 2 (over core).
Axes of the slice: x: 2, y: 2, z: 4, core: 2. Of those that a mesh axis runs over, the one named last changes fastest.
Arguments:
- load_current: float32 [8, 64, 2048], P('layer', 'gx', 'gy'), may hold values from -12 to 12
- pad_cond: float32 [8, 64, 2048], P('layer', 'gx', 'gy'), may hold values from 0.01 to 0.1
- cond_x: float32 [8, 64, 2048], P('layer', 'gx', 'gy'), may hold values from 0.5 to 4
- cond_y: float32 [8, 64, 2048], P('layer', 'gx', 'gy'), may hold values from 0.5 to 4
- via_map: int32 [8, 64, 2048], P('layer', 'gx', 'gy'), may hold values from 0 to 3
- branch_index: int32 [4096, 256], P(('gx', 'gy', 'layer')), may hold values from 0 to 7679
- tree_owner: int32 [4096, 1], P(('gx', 'gy', 'layer')), may hold values from 0 to 15; in each aligned block of 128 rows (0 to 127, 128 to 255, ...) at most 16 rows name the same one
- initial_stress: float32 [4096, 256], P(('gx', 'gy', 'layer')), may hold values from -6 to 6
- block_inverse: float32 [16, 256, 256], P(('gx', 'gy')), may hold values from -1.5 to 1.5
Outputs:
- drop: float32 [8, 64, 2048], P('layer', 'gx', 'gy')
- final_stress: float32 [4096, 256], P(('gx', 'gy', 'layer'))
Inputs may be any that keep to these rules, and one draw needn't show every extreme that they name: `tree_owner`: among the 128 trees of one device at most 16 have one owner, and some owner has exactly 16. Owners count in gx+gy order within the tree's own layer group. `branch_index`: A branch joins a node to its next node along x inside the home tile.
All inputs are finite; a program needn't handle non-finite values.
Results may differ from a plain program's by a relative error of at most 0.0003.
Values sent between devices are 32-bit elements; how exact they have to be, the bound alone decides.
A program may use at most 64 MiB of HBM per device.

v0:
```python
import jax
import jax.numpy as jnp
from jax import lax
from jax.sharding import PartitionSpec as P

KX = 2
KY = 4
ITERS = 2
SWEEPS = 4
STEPS = 8
OMEGA = 0.7
TAU = 0.6
VIA_G = 1.5
COARSE_G = 64.0
KAPPA = 2.0


def padded_2(block, sides, width):
    for axis, dim in sides:
        count = lax.axis_size(axis)
        forward = [(i, i + 1) for i in range(count - 1)]
        backward = [(target, source) for source, target in forward]
        low = lax.ppermute(
            lax.slice_in_dim(block, block.shape[dim] - width, None, axis=dim), axis, forward
        )
        high = lax.ppermute(lax.slice_in_dim(block, 0, width, axis=dim), axis, backward)
        block = jnp.concatenate([low, block, high], axis=dim)
    return block


def grid_rims(stacked):
    return padded_2(stacked, (("gx", 2), ("gy", 3), ("layer", 1)), 1)


def total(values):
    return lax.psum(values, ("gx", "gy", "layer"))


def per_device(
    load_current,
    pad_cond,
    cond_x,
    cond_y,
    via_map,
    branch_index,
    tree_owner,
    initial_stress,
    block_inverse,
):
    layers, rows, cols = load_current.shape
    size_x = lax.axis_size("gx")
    size_y = lax.axis_size("gy")
    size_l = lax.axis_size("layer")
    glob_i = lax.axis_index("gx") * rows + jnp.arange(rows, dtype=jnp.int32)
    glob_j = lax.axis_index("gy") * cols + jnp.arange(cols, dtype=jnp.int32)
    glob_l = lax.axis_index("layer") * layers + jnp.arange(layers, dtype=jnp.int32)
    mask_x = (glob_i < rows * size_x - 1).astype(jnp.float32)
    mask_y = (glob_j < cols * size_y - 1).astype(jnp.float32)
    mask_z = (glob_l < layers * size_l - 1).astype(jnp.float32)
    link_x = cond_x * mask_x[None, :, None]
    link_y = cond_y * mask_y[None, None, :]
    link_z = via_map.astype(jnp.float32) * VIA_G * mask_z[:, None, None]
    links = grid_rims(jnp.stack([link_x, link_y, link_z]))
    down_x = links[0, 1:-1, :-2, 1:-1]
    down_y = links[1, 1:-1, 1:-1, :-2]
    down_z = links[2, :-2, 1:-1, 1:-1]
    diag = pad_cond + link_x + down_x + link_y + down_y + link_z + down_z

    def restrict(field):
        return jnp.sum(field.reshape(layers, KX, rows // KX, KY, cols // KY), axis=(0, 2, 4))

    def prolong(coarse):
        spread = jnp.broadcast_to(
            coarse[None, :, None, :, None], (layers, KX, rows // KX, KY, cols // KY)
        )
        return spread.reshape(layers, rows, cols)

    cdiag_own = restrict(pad_cond)

    def collect(small):
        every = lax.all_gather(small.reshape(1, KX * KY), ("gx", "gy", "layer"), axis=0, tiled=True)
        shaped = every.reshape(size_x, size_y, size_l, KX, KY).transpose(2, 0, 3, 1, 4)
        return shaped.reshape(size_l, size_x * KX, size_y * KY)

    cdiag_all = collect(cdiag_own)
    cdiag_full = cdiag_all + 6.0 * COARSE_G

    def coarse_solve(coarse_rhs):
        rhs_all = collect(coarse_rhs)
        value = jnp.zeros_like(rhs_all)
        for sweep in range(SWEEPS):
            padded = jnp.pad(value, 1)
            beside_all = padded[:-2, 1:-1, 1:-1] + padded[2:, 1:-1, 1:-1]
            beside_all = beside_all + padded[1:-1, 2:, 1:-1] + padded[1:-1, :-2, 1:-1]
            beside_all = beside_all + padded[1:-1, 1:-1, 2:] + padded[1:-1, 1:-1, :-2]
            value = (
                value + TAU * (rhs_all - (cdiag_full * value - COARSE_G * beside_all)) / cdiag_full
            )
        start = (lax.axis_index("layer"), lax.axis_index("gx") * KX, lax.axis_index("gy") * KY)
        return lax.dynamic_slice(value, start, (1, KX, KY))[0]

    def precondition(resid):
        return OMEGA * resid / diag + prolong(coarse_solve(restrict(resid)))

    drop = jnp.zeros_like(load_current)
    resid = load_current
    zvec = precondition(resid)
    direction = zvec
    rz_now = total(jnp.sum(resid * zvec))
    for step in range(ITERS):
        operate_padded = grid_rims(direction[None])[0]
        out = pad_cond * direction
        out = (
            out
            + link_x * (direction - operate_padded[1:-1, 2:, 1:-1])
            + down_x * (direction - operate_padded[1:-1, :-2, 1:-1])
        )
        out = (
            out
            + link_y * (direction - operate_padded[1:-1, 1:-1, 2:])
            + down_y * (direction - operate_padded[1:-1, 1:-1, :-2])
        )
        out = (
            out
            + link_z * (direction - operate_padded[2:, 1:-1, 1:-1])
            + down_z * (direction - operate_padded[:-2, 1:-1, 1:-1])
        )
        alpha = rz_now / total(jnp.sum(direction * out))
        drop = drop + alpha * direction
        resid = resid - alpha * out
        if step + 1 < ITERS:
            zvec = precondition(resid)
            rz_next = total(jnp.sum(resid * zvec))
            direction = zvec + rz_next / rz_now * direction
            rz_now = rz_next
    trees_dev, segs = initial_stress.shape
    owners_count = size_x * size_y
    capacity = 2 * trees_dev // owners_count
    seg_layer = (jnp.arange(segs, dtype=jnp.int32) % layers)[None, :]
    cell = seg_layer * (rows * cols) + branch_index
    flat_drop = drop.reshape(-1)
    flat_link = link_x.reshape(-1)
    current = flat_link[cell] * (flat_drop[cell] - flat_drop[cell + cols])
    owners = tree_owner[:, 0]
    hits = (owners[:, None] == jnp.arange(owners_count, dtype=jnp.int32)[None, :]).astype(jnp.int32)
    slot_rank = jnp.sum((jnp.cumsum(hits, axis=0) - hits) * hits, axis=1)
    payload = jnp.stack([current, initial_stress])
    outgoing = (
        jnp.zeros((2, owners_count, capacity, segs), jnp.float32)
        .at[:, owners, slot_rank]
        .set(payload)
    )
    inverse = block_inverse[0]
    piece = lax.all_to_all(outgoing, ("gx", "gy"), split_axis=1, concat_axis=1, tiled=True)
    count = piece.shape[2]
    flow = piece[0].reshape(-1, segs)
    stress = piece[1].reshape(-1, segs)
    for step in range(STEPS):
        stress = jnp.einsum(
            "ts,us->tu", stress + KAPPA * flow, inverse, precision=lax.Precision.HIGHEST
        )
    returning = stress.reshape(owners_count, count, segs)
    solved = lax.all_to_all(returning, ("gx", "gy"), split_axis=0, concat_axis=0, tiled=True)
    final_stress = solved[owners, slot_rank]
    return (drop, final_stress)


def solution(mesh):
    return jax.shard_map(
        per_device,
        mesh=mesh,
        in_specs=(
            P("layer", "gx", "gy"),
            P("layer", "gx", "gy"),
            P("layer", "gx", "gy"),
            P("layer", "gx", "gy"),
            P("layer", "gx", "gy"),
            P(("gx", "gy", "layer"), None),
            P(("gx", "gy", "layer"), None),
            P(("gx", "gy", "layer"), None),
            P(("gx", "gy"), None, None),
        ),
        out_specs=(P("layer", "gx", "gy"), P(("gx", "gy", "layer"), None)),
        check_vma=False,
    )
```

profile of v0, /device:TPU:0, one launch (start us, length us, event | category | flops | bytes accessed | tf_op | source)
XLA Modules:
  0.0 902.8 jit_solution(7220110713637692259)
XLA Ops:
  1.9 4.9 collective-permute-start
  6.9 1.3 collective-permute-start.1
  8.4 42.6 %all-gather.1 = f32[32,1,8]{2,1,0:T(1,128)S(1)} all-gather(f32[1,1,8]{2,1,0:T(1,128)S(1)} %reshape.172), channel_id=1, replica_groups=mesh['gx'=4,'gy'=4,'layer'=2] {'gx','gy','layer'}, dimensions={0}, use_global_device_ids=true | all-gather | bytes 1056 | tf_op jit(solution)/shard_map/all_gather | solution.py:81
  51.5 36.4 %all-gather = f32[32,1,8]{2,1,0:T(1,128)S(1)} all-gather(f32[1,1,8]{2,1,0:T(1,128)S(1)} %reshape.170), channel_id=1, replica_groups=mesh['gx'=4,'gy'=4,'layer'=2] {'gx','gy','layer'}, dimensions={0}, use_global_device_ids=true | all-gather | bytes 1056 | tf_op jit(solution)/shard_map/all_gather | solution.py:81
  90.3 3.6 collective-permute-start.2
  95.3 2.2 collective-permute-done.2
  97.5 4.1 collective-permute-done.3
  101.8 1.3 collective-permute-start.4
  107.0 4.1 collective-permute-done.6
  111.2 3.2 collective-permute-start.7
  116.2 4.3 collective-permute-done.8
  120.6 1.3 collective-permute-start.10
  121.9 3.0 collective-permute-start.9
  126.9 39.2 %all-reduce.7 = (f32[]{:T(128)}, f32[]{:T(128)}) all-reduce(f32[]{:T(128)} %get-tuple-element.3, f32[]{:T(128)} %get-tuple-element.2), channel_id=1, replica_groups=mesh['gx'=4,'gy'=4,'layer'=2] {'gx','gy','layer'}, use_global_device_ids=true, to_apply=%region_5.6 | all-reduce | flops 2 | bytes 16 | tf_op jit(solution)/shard_map/psum | solution.py:36
  167.6 41.0 %all-gather.2 = f32[32,1,8]{2,1,0:T(1,128)S(1)} all-gather(f32[1,1,8]{2,1,0:T(1,128)S(1)} %reshape.174), channel_id=1, replica_groups=mesh['gx'=4,'gy'=4,'layer'=2] {'gx','gy','layer'}, dimensions={0}, use_global_device_ids=true | all-gather | bytes 1056 | tf_op jit(solution)/shard_map/all_gather | solution.py:81
  210.7 37.1 %psum.30 = f32[]{:T(128)} all-reduce(f32[]{:T(128)} %get-tuple-element.8), channel_id=1, replica_groups=mesh['gx'=4,'gy'=4,'layer'=2] {'gx','gy','layer'}, use_global_device_ids=true, to_apply=%region_11.12 | all-reduce | flops 1 | bytes 8 | tf_op jit(solution)/shard_map/psum | solution.py:36
  249.0 4.8 collective-permute-start.11
  253.8 1.3 collective-permute-start.12
  255.4 4.0 collective-permute-done.12
  259.4 4.2 collective-permute-start.13
  263.6 1.3 collective-permute-start.14
  265.4 4.3 collective-permute-done.14
  269.7 1.3 collective-permute-start.15
  272.4 1.8 collective-permute-done.16
  275.2 180.5 %gather_fusion = f32[32768]{0:T(1024)S(1)} fusion(f32[32768]{0:T(1024)S(1)} %bitcast.94, s32[32768]{0:T(1024)S(1)} %broadcast_clamp_fusion.1), kind=kCustom, calls=%fused_computation | custom fusion | bytes 393216 | tf_op jit(solution)/shard_map/gather | solution.py:143
  455.8 39.4 %psum.31 = f32[]{:T(128)} all-reduce(f32[]{:T(128)} %fusion.22), channel_id=1, replica_groups=mesh['gx'=4,'gy'=4,'layer'=2] {'gx','gy','layer'}, use_global_device_ids=true, to_apply=%region_13.14 | all-reduce | flops 1 | bytes 8 | tf_op jit(solution)/shard_map/psum | solution.py:36
  497.2 180.5 %gather_fusion.1 = f32[32768]{0:T(1024)S(1)} fusion(f32[32768]{0:T(1024)S(1)} %bitcast.92, s32[32768]{0:T(1024)S(1)} %broadcast_clamp_fusion.1), kind=kCustom, calls=%fused_computation.1 | custom fusion | bytes 393216 | tf_op jit(solution)/shard_map/gather | solution.py:143
  677.7 180.5 %gather_fusion.2 = f32[32768]{0:T(1024)S(1)} fusion(f32[32768]{0:T(1024)S(1)} %bitcast.93, s32[32768]{0:T(1024)S(1)} %broadcast_clamp_fusion), kind=kCustom, calls=%fused_computation.2 | custom fusion | bytes 393216 | tf_op jit(solution)/shard_map/gather | solution.py:143
  859.6 5.7 scatter_fusion
  865.4 19.4 %all_to_all.10 = f32[2,16,16,256]{3,0,2,1:T(2,128)S(1)} all-to-all(f32[2,16,16,256]{3,0,2,1:T(2,128)S(1)} %scatter_fusion), channel_id=1, replica_groups=mesh['gx'=4,'gy'=4,'layer'=2] {'gx','gy'}, dimensions={1} | all-to-all | bytes 1048576 | tf_op jit(solution)/shard_map/all_to_all | solution.py:154
  888.7 12.1 %all_to_all.11 = f32[16,16,256]{2,1,0:T(8,128)S(1)} all-to-all(f32[16,16,256]{2,1,0:T(8,128)S(1)} %fusion), channel_id=1, replica_groups=mesh['gx'=4,'gy'=4,'layer'=2] {'gx','gy'}, dimensions={0} | all-to-all | bytes 524288 | tf_op jit(solution)/shard_map/all_to_all | solution.py:163
  900.9 1.9 gather_fusion.3
  (121 shorter events, 25.0 us)
Async XLA Ops:
  0.6 884.7 %copy-start = (f32[1,256,256]{2,1,0:T(8,128)S(1)}, f32[1,256,256]{2,1,0:T(8,128)}, u32[]{:S(2)}) copy-start(f32[1,256,256]{2,1,0:T(8,128)} %param.17) | copy-start | bytes 786436
  0.7 1.1 copy-start.4
  0.7 1.1 copy-start.5
  1.9 6.3 copy-start.3
  1.9 88.2 %collective-permute-start = (f32[3,4,1,512]{3,2,1,0:T(1,128)S(1)}, f32[3,4,1,512]{3,2,1,0:T(1,128)S(1)}, u32[]{:S(2)}, u32[]{:S(2)}) collective-permute-start(f32[3,4,1,512]{3,2,1,0:T(1,128)S(1)} %get-tuple-element.23), channel_id=1, source_target_pairs={{0,8},{8,16},{16,24},{1,9},{9,17},{17,25},{2,10},{10,18},{18,26},{... | collective-permute-start | bytes 73736 | tf_op jit(solution)/shard_map/ppermute | solution.py:23
  6.9 83.3 %collective-permute-start.1 = (f32[3,4,1,512]{3,2,1,0:T(1,128)S(1)}, f32[3,4,1,512]{3,2,1,0:T(1,128)S(1)}, u32[]{:S(2)}, u32[]{:S(2)}) collective-permute-start(f32[3,4,1,512]{3,2,1,0:T(1,128)S(1)} %get-tuple-element.22), channel_id=1, source_target_pairs={{8,0},{16,8},{24,16},{9,1},{17,9},{25,17},{10,2},{18,10},{26,18},{... | collective-permute-start | bytes 73736 | tf_op jit(solution)/shard_map/ppermute | solution.py:26
  8.2 43.1 %copy-start.2 = (f32[4,16,512]{2,1,0:T(8,128)S(1)}, f32[4,16,512]{2,1,0:T(8,128)}, u32[]{:S(2)}) copy-start(f32[4,16,512]{2,1,0:T(8,128)} %param.9) | copy-start | bytes 393220
  89.1 0.9 copy-start.7
  90.3 7.2 collective-permute-start.2
  93.9 7.7 collective-permute-start.3
  101.8 2.3 collective-permute-start.4
  103.1 1.0 copy-start.1
  104.3 2.7 collective-permute-start.5
  105.6 5.6 collective-permute-start.6
  111.2 4.9 collective-permute-start.7
  114.5 6.0 collective-permute-start.8
  120.6 4.4 collective-permute-start.10
  121.9 3.9 collective-permute-start.9
  249.0 6.4 collective-permute-start.11
  253.8 1.3 copy-start.9
  253.8 5.5 collective-permute-start.12
  259.4 5.9 collective-permute-start.13
  263.6 6.0 collective-permute-start.14
  269.7 2.7 collective-permute-start.15
  271.0 3.1 collective-permute-start.16
  496.5 0.7 copy-start.6
  858.3 0.9 copy-start.8
where the time goes:
time: 904 us; the launch traced here: 903 us
  local copies, waits for them, and re-layouts  553 us (61%)
  blocking collectives  267 us (30%)
  starting transfers between devices  38 us (4%)
  waiting for transfers between devices  27 us (3%)
    gather x3, local copies, waits for them, and re-layouts, per_device(): current = flat_link[cell] * (flat_drop[cell] - flat_drop[cell + cols])  542 us
    all_gather x3, blocking collectives, collect(): lax.all_gather(small.reshape(1, KX * KY), ('gx', 'gy', 'layer'), axis=0,...  120 us
    psum x3, blocking collectives, total(): return lax.psum(values, ('gx', 'gy', 'layer'))  116 us
    ppermute x9, starting transfers between devices, padded_2(): lax.ppermute(lax.slice_in_dim(block, block.shape[dim] - width, None, axis...  27.6 us
    ppermute x8, waiting for transfers between devices, padded_2(): lax.ppermute(lax.slice_in_dim(block, 0, width, axis=dim), axis, backward)  22.5 us
    all_to_all x1, blocking collectives, per_device(): lax.all_to_all(outgoing, ('gx', 'gy'), split_axis=1, concat_axis=1, tiled...  19.4 us
  transfers between devices with their start and end apart: 17, of which 11 were waited for; matrix products, arithmetic and copies ran while one was open for 0% of the time, Pallas kernels for 0%

commit v1 on v0

--- a/solution.py
+++ b/solution.py
@@ -33,7 +33,7 @@
 
 
 def total(values):
-    return lax.psum(values, ("gx", "gy", "layer"))
+    return jax.lax.psum(jax.lax.psum(values, ("gy", "layer")), "gx")
 
 
 def per_device(

time: 904 us -> 847 us (0.937)
  blocking collectives: 267 us -> 214 us
    psum x3 -> x6, blocking collectives: 116 us -> 68 us  [total(): return jax.lax.psum(jax.lax.psum(values, ('gy', 'layer')), 'gx')]
where the time goes in v1:
time: 847 us
  local copies, waits for them, and re-layouts  553 us (65%)
  blocking collectives  214 us (25%)
  starting transfers between devices  33.3 us (4%)
  waiting for transfers between devices  29 us (3%)
  other arithmetic  8.71 us (1%)
    gather x3, local copies, waits for them, and re-layouts, per_device(): current = flat_link[cell] * (flat_drop[cell] - flat_drop[cell + cols])  542 us
    all_gather x3, blocking collectives, collect(): lax.all_gather(small.reshape(1, KX * KY), ('gx', 'gy', 'layer'), axis=0,...  116 us
    psum x6, blocking collectives, total(): return jax.lax.psum(jax.lax.psum(values, ('gy', 'layer')), 'gx')  68 us
    ppermute x8, waiting for transfers between devices, padded_2(): lax.ppermute(lax.slice_in_dim(block, 0, width, axis=dim), axis, backward)  24.4 us
    ppermute x9, starting transfers between devices, padded_2(): lax.ppermute(lax.slice_in_dim(block, block.shape[dim] - width, None, axis...  23 us
    all_to_all x1, blocking collectives, per_device(): lax.all_to_all(outgoing, ('gx', 'gy'), split_axis=1, concat_axis=1, tiled...  18.3 us
  transfers between devices with their start and end apart: 17, of which 11 were waited for; matrix products, arithmetic and copies ran while one was open for 0% of the time, Pallas kernels for 0%

profile of v1, /device:TPU:0, one launch (start us, length us, event | category | flops | bytes accessed | tf_op | source)
XLA Modules:
  0.0 846.6 jit_solution(3146672086973170022)
XLA Ops:
  1.9 4.9 collective-permute-start
  8.4 42.6 %all-gather.1 = f32[32,1,8]{2,1,0:T(1,128)S(1)} all-gather(f32[1,1,8]{2,1,0:T(1,128)S(1)} %reshape.172), channel_id=1, replica_groups=mesh['gx'=4,'gy'=4,'layer'=2] {'gx','gy','layer'}, dimensions={0}, use_global_device_ids=true | all-gather | bytes 1056 | tf_op jit(solution)/shard_map/all_gather | solution.py:81
  51.5 36.4 %all-gather = f32[32,1,8]{2,1,0:T(1,128)S(1)} all-gather(f32[1,1,8]{2,1,0:T(1,128)S(1)} %reshape.170), channel_id=1, replica_groups=mesh['gx'=4,'gy'=4,'layer'=2] {'gx','gy','layer'}, dimensions={0}, use_global_device_ids=true | all-gather | bytes 1056 | tf_op jit(solution)/shard_map/all_gather | solution.py:81
  89.9 3.6 collective-permute-start.2
  94.9 2.2 collective-permute-done.2
  97.1 4.1 collective-permute-done.3
  101.3 1.3 collective-permute-start.4
  106.6 4.1 collective-permute-done.6
  110.8 3.2 collective-permute-start.7
  115.8 4.3 collective-permute-done.8
  121.5 3.0 collective-permute-start.9
  126.4 12.9 %all-reduce.7 = (f32[]{:T(128)}, f32[]{:T(128)}) all-reduce(f32[]{:T(128)} %get-tuple-element.3, f32[]{:T(128)} %get-tuple-element.2), channel_id=1, replica_groups=mesh['gx'=4,'gy'=4,'layer'=2] {'gy','layer'}, use_global_device_ids=true, to_apply=%region_5.6 | all-reduce | flops 2 | bytes 16 | tf_op jit(solution)/shard_map/psum | solution.py:36
  139.3 10.2 %all-reduce.8 = (f32[]{:T(128)}, f32[]{:T(128)}) all-reduce(f32[]{:T(128)} %get-tuple-element.4, f32[]{:T(128)} %get-tuple-element.5), channel_id=1, replica_groups=mesh['gx'=4,'gy'=4,'layer'=2] {'gx'}, use_global_device_ids=true, to_apply=%region_6.7 | all-reduce | flops 2 | bytes 16 | tf_op jit(solution)/shard_map/psum | solution.py:36
  151.0 36.7 %all-gather.2 = f32[32,1,8]{2,1,0:T(1,128)S(1)} all-gather(f32[1,1,8]{2,1,0:T(1,128)S(1)} %reshape.174), channel_id=1, replica_groups=mesh['gx'=4,'gy'=4,'layer'=2] {'gx','gy','layer'}, dimensions={0}, use_global_device_ids=true | all-gather | bytes 1056 | tf_op jit(solution)/shard_map/all_gather | solution.py:81
  189.7 12.7 %psum.60 = f32[]{:T(128)} all-reduce(f32[]{:T(128)} %get-tuple-element.10), channel_id=1, replica_groups=mesh['gx'=4,'gy'=4,'layer'=2] {'gy','layer'}, use_global_device_ids=true, to_apply=%region_13.14 | all-reduce | flops 1 | bytes 8 | tf_op jit(solution)/shard_map/psum | solution.py:36
  202.4 10.6 %psum.61 = f32[]{:T(128)} all-reduce(f32[]{:T(128)} %psum.60), channel_id=1, replica_groups=mesh['gx'=4,'gy'=4,'layer'=2] {'gx'}, use_global_device_ids=true, to_apply=%region_14.15 | all-reduce | flops 1 | bytes 8 | tf_op jit(solution)/shard_map/psum | solution.py:36
  214.4 2.3 collective-permute-start.11
  216.7 1.3 collective-permute-start.12
  218.2 4.0 collective-permute-done.12
  222.3 2.0 collective-permute-start.13
  226.1 6.1 collective-permute-done.14
  232.3 1.3 collective-permute-start.15
  234.9 1.8 collective-permute-done.16
  237.8 12.6 %psum.62 = f32[]{:T(128)} all-reduce(f32[]{:T(128)} %fusion.22), channel_id=1, replica_groups=mesh['gx'=4,'gy'=4,'layer'=2] {'gy','layer'}, use_global_device_ids=true, to_apply=%region_16.17 | all-reduce | flops 1 | bytes 8 | tf_op jit(solution)/shard_map/psum | solution.py:36
  250.4 180.5 %gather_fusion = f32[32768]{0:T(1024)S(1)} fusion(f32[32768]{0:T(1024)S(1)} %bitcast.94, s32[32768]{0:T(1024)S(1)} %broadcast_clamp_fusion.1), kind=kCustom, calls=%fused_computation | custom fusion | bytes 393216 | tf_op jit(solution)/shard_map/gather | solution.py:143
  430.9 9.0 %psum.63 = f32[]{:T(128)} all-reduce(f32[]{:T(128)} %psum.62), channel_id=1, replica_groups=mesh['gx'=4,'gy'=4,'layer'=2] {'gx'}, use_global_device_ids=true, to_apply=%region_17.18 | all-reduce | flops 1 | bytes 8 | tf_op jit(solution)/shard_map/psum | solution.py:36
  442.0 180.5 %gather_fusion.1 = f32[32768]{0:T(1024)S(1)} fusion(f32[32768]{0:T(1024)S(1)} %bitcast.92, s32[32768]{0:T(1024)S(1)} %broadcast_clamp_fusion.1), kind=kCustom, calls=%fused_computation.1 | custom fusion | bytes 393216 | tf_op jit(solution)/shard_map/gather | solution.py:143
  622.5 180.5 %gather_fusion.2 = f32[32768]{0:T(1024)S(1)} fusion(f32[32768]{0:T(1024)S(1)} %bitcast.93, s32[32768]{0:T(1024)S(1)} %broadcast_clamp_fusion), kind=kCustom, calls=%fused_computation.2 | custom fusion | bytes 393216 | tf_op jit(solution)/shard_map/gather | solution.py:143
  804.5 5.7 scatter_fusion
  810.2 18.3 %all_to_all.10 = f32[2,16,16,256]{3,0,2,1:T(2,128)S(1)} all-to-all(f32[2,16,16,256]{3,0,2,1:T(2,128)S(1)} %scatter_fusion), channel_id=1, replica_groups=mesh['gx'=4,'gy'=4,'layer'=2] {'gx','gy'}, dimensions={1} | all-to-all | bytes 1048576 | tf_op jit(solution)/shard_map/all_to_all | solution.py:154
  832.5 12.2 %all_to_all.11 = f32[16,16,256]{2,1,0:T(8,128)S(1)} all-to-all(f32[16,16,256]{2,1,0:T(8,128)S(1)} %fusion), channel_id=1, replica_groups=mesh['gx'=4,'gy'=4,'layer'=2] {'gx','gy'}, dimensions={0} | all-to-all | bytes 524288 | tf_op jit(solution)/shard_map/all_to_all | solution.py:163
  844.7 1.9 gather_fusion.3
  (124 shorter events, 28.5 us)
Async XLA Ops:
  0.6 828.5 %copy-start = (f32[1,256,256]{2,1,0:T(8,128)S(1)}, f32[1,256,256]{2,1,0:T(8,128)}, u32[]{:S(2)}) copy-start(f32[1,256,256]{2,1,0:T(8,128)} %param.17) | copy-start | bytes 786436
  0.7 1.1 copy-start.4
  0.7 1.1 copy-start.5
  1.9 6.3 copy-start.3
  1.9 87.8 %collective-permute-start = (f32[3,4,1,512]{3,2,1,0:T(1,128)S(1)}, f32[3,4,1,512]{3,2,1,0:T(1,128)S(1)}, u32[]{:S(2)}, u32[]{:S(2)}) collective-permute-start(f32[3,4,1,512]{3,2,1,0:T(1,128)S(1)} %get-tuple-element.25), channel_id=1, source_target_pairs={{0,8},{8,16},{16,24},{1,9},{9,17},{17,25},{2,10},{10,18},{18,26},{... | collective-permute-start | bytes 73736 | tf_op jit(solution)/shard_map/ppermute | solution.py:23
  6.9 82.9 %collective-permute-start.1 = (f32[3,4,1,512]{3,2,1,0:T(1,128)S(1)}, f32[3,4,1,512]{3,2,1,0:T(1,128)S(1)}, u32[]{:S(2)}, u32[]{:S(2)}) collective-permute-start(f32[3,4,1,512]{3,2,1,0:T(1,128)S(1)} %get-tuple-element.24), channel_id=1, source_target_pairs={{8,0},{16,8},{24,16},{9,1},{17,9},{25,17},{10,2},{18,10},{26,18},{... | collective-permute-start | bytes 73736 | tf_op jit(solution)/shard_map/ppermute | solution.py:26
  8.2 43.1 %copy-start.2 = (f32[4,16,512]{2,1,0:T(8,128)S(1)}, f32[4,16,512]{2,1,0:T(8,128)}, u32[]{:S(2)}) copy-start(f32[4,16,512]{2,1,0:T(8,128)} %param.9) | copy-start | bytes 393220
  89.9 7.2 collective-permute-start.2
  93.5 7.7 collective-permute-start.3
  94.9 8.8 %copy-start.1 = (f32[4,16,512]{2,1,0:T(8,128)S(1)}, f32[4,16,512]{2,1,0:T(8,128)}, u32[]{:S(2)}) copy-start(f32[4,16,512]{2,1,0:T(8,128)} %param.11) | copy-start | bytes 393220
  101.3 2.3 collective-permute-start.4
  102.7 3.8 copy-start.7
  103.9 2.7 collective-permute-start.5
  105.2 5.6 collective-permute-start.6
  110.8 4.9 collective-permute-start.7
  114.0 6.0 collective-permute-start.8
  120.2 4.4 collective-permute-start.10
  121.5 3.9 collective-permute-start.9
  214.4 3.9 collective-permute-start.11
  216.6 1.3 copy-start.9
  216.7 5.5 collective-permute-start.12
  222.3 3.8 collective-permute-start.13
  224.3 7.8 collective-permute-start.14
  232.3 2.6 collective-permute-start.15
  233.6 3.1 collective-permute-start.16
  441.3 0.7 copy-start.6
  803.1 0.9 copy-start.8
